TPU v7x, 512 devices: a whole 4x4x16 slice. The times are simulated.
512 devices in a mesh: tile: 128 (over y, z, core), fit: 4 (over x).
Axes of the slice: x: 4, y: 4, z: 16, core: 2. Of those that a mesh axis runs over, the one named last changes fastest.
Arguments:
- factors: bfloat16 [128, 128, 128, 128], P('tile', 'fit'), may hold values from -0.21875 to 0.21875
- amplitudes: bfloat16 [256, 128, 128], P('tile'), may hold values from -6 to 6
- left_step: int32 [256, 13], P('tile'), may hold values from -1 to 1
- right_step: int32 [256, 13], P('tile'), may hold values from -1 to 1
- amp_owner: int32 [256, 13], P('tile'), may hold values from 0 to 127, all different within a row; in each aligned block of 2 rows (0 to 1, 2 to 3, ...) no two rows name the same one
- amp_slot: int32 [256, 13], P('tile'), may hold values from 0 to 1
Outputs:
- residual: bfloat16 [256, 128, 128], P('tile', 'fit')
Inputs may be any that keep to these rules, and one draw needn't show every extreme that they name: `amp_owner`: among the 13 terms of the 2 residual tiles of one device, no owner index is named more than 1 times, a bound that some block reaches.
All inputs are finite; a program needn't handle non-finite values.
Results may differ from a plain program's by a relative error of at most 0.0049.
Values may be sent and summed in bfloat16 or wider, within the bound.
A program may use at most 64 MiB of HBM per device.

v0:
```python
import jax
import jax.numpy as jnp
from jax import lax
from jax.sharding import PartitionSpec as P


def padded(cells, sides, width):
    for axis, dim in sides:
        count = lax.axis_size(axis)
        ends = count - 1
        head = lax.slice_in_dim(cells, 0, width, axis=dim)
        tail = lax.slice_in_dim(cells, cells.shape[dim] - width, cells.shape[dim], axis=dim)
        cells = jnp.concatenate(
            [
                lax.ppermute(tail, axis, [(i, (i + 1) % count) for i in range(ends)]),
                cells,
                lax.ppermute(head, axis, [((i + 1) % count, i) for i in range(ends)]),
            ],
            axis=dim,
        )
    return cells


def body(factors, amplitudes, left_step, right_step, amp_owner, amp_slot):
    tiles = lax.axis_size("tile")
    here = lax.axis_index("tile")
    nz_dev = amplitudes.shape[0]
    width = amplitudes.shape[1]
    terms = left_step.shape[1]
    count = nz_dev * terms
    rims = padded(factors, (("tile", 0),), 1)
    left_pos = jnp.clip(here + left_step.reshape(count), 0, tiles - 1) - here + 1
    right_pos = jnp.clip(here + right_step.reshape(count), 0, tiles - 1) - here + 1
    owners = amp_owner.reshape(count)
    slots = amp_slot.reshape(count)
    wanted = owners * nz_dev + slots
    piece = lax.all_gather(amplitudes, "tile", axis=0, tiled=True)
    rows = piece.shape[0]
    marks = (wanted[:, None] == jnp.arange(rows)[None, :]).astype(jnp.bfloat16)
    picked = jnp.dot(marks, piece.reshape(rows, width * width), preferred_element_type=jnp.float32)
    picked = picked.astype(jnp.bfloat16).reshape(count, width, width)

    def add_term(index, total):
        right_fac = lax.dynamic_index_in_dim(rims, right_pos[index], 0, keepdims=False)
        left_fac = lax.dynamic_index_in_dim(rims, left_pos[index], 0, keepdims=False)
        ampl = lax.dynamic_index_in_dim(picked, index, 0, keepdims=False)
        half = jnp.einsum(
            "cd,pbd->pcb", ampl, right_fac, preferred_element_type=jnp.float32
        ).astype(jnp.bfloat16)
        term = jnp.einsum("pac,pcb->ab", left_fac, half, preferred_element_type=jnp.float32)
        return total.at[index // terms].add(term)

    partial_sums = lax.fori_loop(0, count, add_term, jnp.zeros((nz_dev, width, width), jnp.float32))
    return lax.psum_scatter(partial_sums, "fit", scatter_dimension=1, tiled=True).astype(
        jnp.bfloat16
    )


def solution(mesh):
    return jax.shard_map(
        body,
        mesh=mesh,
        in_specs=(
            P("tile", "fit", None, None),
            P("tile", None, None),
            P("tile", None),
            P("tile", None),
            P("tile", None),
            P("tile", None),
        ),
        out_specs=P("tile", "fit", None),
        check_vma=False,
    )
```

profile of v0, /device:TPU:1, one launch (start us, length us, event | category | flops | bytes accessed | tf_op | source)
XLA Modules:
  0.0 388.8 jit_solution(2627662496836380038)
XLA Ops:
  6.5 0.7 all-gather.2.cloned.1.call-update
  7.3 4.9 %collective-permute-start = (bf16[1,32,128,128]{3,2,1,0:T(8,128)(2,1)}, bf16[1,32,128,128]{3,2,1,0:T(8,128)(2,1)S(1)}, u32[]{:S(2)}, u32[]{:S(2)}) collective-permute-start(bf16[1,32,128,128]{3,2,1,0:T(8,128)(2,1)} %param.10), channel_id=1, source_target_pairs={{0,4},{4,8},{8,12},{12,16},{16,20},{20,24},{24,28},{28,32},{32,36}... | collective-permute-start | bytes 3145736 | tf_op jit(solution)/shard_map/ppermute | solution.py:15
  12.2 5.2 %collective-permute-start.1 = (bf16[1,32,128,128]{3,2,1,0:T(8,128)(2,1)}, bf16[1,32,128,128]{3,2,1,0:T(8,128)(2,1)}, u32[]{:S(2)}, u32[]{:S(2)}) collective-permute-start(bf16[1,32,128,128]{3,2,1,0:T(8,128)(2,1)} %param.10), channel_id=1, source_target_pairs={{4,0},{8,4},{12,8},{16,12},{20,16},{24,20},{28,24},{32,28},{36,32}... | collective-permute-start | bytes 3145736 | tf_op jit(solution)/shard_map/ppermute | solution.py:17
  17.5 0.7 multiply_add_fusion
  18.3 0.7 subtract_add_fusion
  19.1 5.2 %collective-permute-done = bf16[1,32,128,128]{3,2,1,0:T(8,128)(2,1)S(1)} collective-permute-done((bf16[1,32,128,128]{3,2,1,0:T(8,128)(2,1)}, bf16[1,32,128,128]{3,2,1,0:T(8,128)(2,1)S(1)}, u32[]{:S(2)}, u32[]{:S(2)}) %collective-permute-start) | collective-permute-done | bytes 1048608 | tf_op jit(solution)/shard_map/ppermute | solution.py:15
  24.3 1.0 copy-done.1
  25.2 3.4 collective-permute-done.1
  28.7 2.2 pad_maximum_fusion
  30.9 132.4 %all-gather.2.cloned.1.call-done = bf16[256,128,128]{2,1,0:T(8,128)(2,1)} async-done(((bf16[2,128,128]{2,1,0:T(8,128)(2,1)}), bf16[256,128,128]{2,1,0:T(8,128)(2,1)}) %all-gather.2.cloned.1.call-update) | async-done | bytes 8388624 | tf_op jit(solution)/shard_map/all_gather | solution.py:37
  163.3 8.1 %convolution_convert_fusion.1 = bf16[26,16384]{1,0:T(8,128)(2,1)S(1)} fusion(bf16[32,8,128,128]{3,2,1,0:T(8,128)(2,1)} %bitcast.59, s32[26]{0:T(128)S(1)} %add.128), kind=kOutput, calls=%fused_computation.15 | convolution fusion | flops 218536448 | bytes 9240680 | tf_op jit(solution)/shard_map/dot_general | solution.py:40
  171.7 1.0 slice.35
  172.6 186.6 %while.16 = (s32[]{:T(128)}, f32[2,128,128]{2,1,0:T(8,128)S(1)}, s32[26]{0:T(128)S(1)}, bf16[3,32,128,128]{3,2,1,0:T(8,128)(2,1)S(1)}, s32[26]{0:T(128)S(1)}, /*...) while((s32[]{:T(128)}, f32[2,128,128]{2,1,0:T(8,128)S(1)}, ...), condition=%wide.region_2.3_spmd, body=%wide.region_0.2_spmd.sunk | while | flops 268992544 | bytes 2262394 | solution.py:53
  177.1 0.7 and_reduce_fusion.2
  177.8 2.0 fusion.28
  184.3 0.7 and_reduce_fusion.2
  185.0 2.0 fusion.28
  191.5 0.7 and_reduce_fusion.2
  192.2 2.0 fusion.28
  198.6 0.7 and_reduce_fusion.2
  199.3 2.0 fusion.28
  205.8 0.7 and_reduce_fusion.2
  206.5 2.0 fusion.28
  213.0 0.7 and_reduce_fusion.2
  213.7 2.0 fusion.28
  220.2 0.7 and_reduce_fusion.2
  220.9 2.0 fusion.28
  227.4 0.7 and_reduce_fusion.2
  228.0 2.0 fusion.28
  234.5 0.7 and_reduce_fusion.2
  235.2 2.0 fusion.28
  241.7 0.7 and_reduce_fusion.2
  242.4 2.0 fusion.28
  248.9 0.7 and_reduce_fusion.2
  249.6 2.0 fusion.28
  256.1 0.7 and_reduce_fusion.2
  256.8 2.0 fusion.28
  263.3 0.7 and_reduce_fusion.2
  263.9 2.0 fusion.28
  270.4 0.7 and_reduce_fusion.2
  271.1 2.0 fusion.28
  277.6 0.7 and_reduce_fusion.2
  278.3 2.0 fusion.28
  284.8 0.7 and_reduce_fusion.2
  285.5 2.0 fusion.28
  292.0 0.7 and_reduce_fusion.2
  292.7 2.0 fusion.28
  299.2 0.7 and_reduce_fusion.2
  299.8 2.0 fusion.28
  306.3 0.7 and_reduce_fusion.2
  307.0 2.0 fusion.28
  313.5 0.7 and_reduce_fusion.2
  314.2 2.0 fusion.28
  321.4 2.0 fusion.28
  327.9 0.7 and_reduce_fusion.2
  328.6 2.0 fusion.28
  335.7 2.0 fusion.28
  342.2 0.7 and_reduce_fusion.2
  342.9 2.0 fusion.28
  349.4 0.7 and_reduce_fusion.2
  350.1 2.0 fusion.28
  357.3 2.0 fusion.28
  360.0 20.6 %reduce-scatter.2.cloned.1.call-done = f32[2,32,128]{2,1,0:T(8,128)} async-done(((f32[2,128,128]{2,1,0:T(8,128)}), f32[2,32,128]{2,1,0:T(8,128)}) %reduce-scatter.2.cloned.1.call-update) | async-done | bytes 32784 | tf_op jit(solution)/shard_map/reduce_scatter | solution.py:54
  380.6 1.4 convert_element_type.21
  (68 shorter events, 32.4 us)
Async XLA Ops:
  6.5 156.7 %all-gather.2.cloned.1.call-start = ((), (), s32[]{:S(2)}) async-start(), calls=%async_computation.1 | async-start | bytes 8454144 | tf_op jit(solution)/shard_map/all_gather | solution.py:37
  7.3 373.4 %reduce-scatter.2.cloned.1.call-start = ((), (), s32[]{:S(2)}) async-start(), calls=%async_computation.2 | async-start | bytes 163840 | tf_op jit(solution)/shard_map/reduce_scatter | solution.py:54
  7.3 17.0 %collective-permute-start = (bf16[1,32,128,128]{3,2,1,0:T(8,128)(2,1)}, bf16[1,32,128,128]{3,2,1,0:T(8,128)(2,1)S(1)}, u32[]{:S(2)}, u32[]{:S(2)}) collective-permute-start(bf16[1,32,128,128]{3,2,1,0:T(8,128)(2,1)} %param.10), channel_id=1, source_target_pairs={{0,4},{4,8},{8,12},{12,16},{16,20},{20,24},{24,28},{28,32},{32,36}... | collective-permute-start | bytes 3145736 | tf_op jit(solution)/shard_map/ppermute | solution.py:15
  12.2 16.4 %collective-permute-start.1 = (bf16[1,32,128,128]{3,2,1,0:T(8,128)(2,1)}, bf16[1,32,128,128]{3,2,1,0:T(8,128)(2,1)}, u32[]{:S(2)}, u32[]{:S(2)}) collective-permute-start(bf16[1,32,128,128]{3,2,1,0:T(8,128)(2,1)} %param.10), channel_id=1, source_target_pairs={{4,0},{8,4},{12,8},{16,12},{20,16},{24,20},{28,24},{32,28},{36,32}... | collective-permute-start | bytes 3145736 | tf_op jit(solution)/shard_map/ppermute | solution.py:17
  24.3 1.0 copy-start.1
  171.4 1.2 copy-start.2
  359.3 0.7 copy-start
Sparse Core Ops, SparseCore 0:
  10.5 152.7 all-gather.1
  360.1 20.4 reduce-scatter.1
where the time goes:
time: 394 us; the launch traced here: 389 us
  waiting for transfers between devices  162 us (41%)
  loops' own time  87.2 us (22%)
  matrix products  60.7 us (15%)
  local copies, waits for them, and re-layouts  32.2 us (8%)
  other arithmetic  22.7 us (6%)
  between operations  13.5 us (3%)
  starting transfers between devices  10.2 us (3%)
    all_gather x1, waiting for transfers between devices, body(): piece = lax.all_gather(amplitudes, 'tile', axis=0, tiled=True)  132 us
    another operation x1, loops' own time, body(): lax.fori_loop(0, count, add_term, jnp.zeros((nz_dev, width, width), jnp.f...  87.2 us
    dot_general x26, matrix products, add_term(): jnp.einsum('pac,pcb->ab', left_fac, half, preferred_element_type=jnp.floa...  52.5 us
    reduce_scatter x1, waiting for transfers between devices, body(): lax.psum_scatter(partial_sums, 'fit', scatter_dimension=1, tiled=True)  20.6 us
    another operation x26, other arithmetic  17.7 us
    dynamic_slice x26, local copies, waits for them, and re-layouts, add_term(): right_pos[index]  14.6 us
    dynamic_slice x26, local copies, waits for them, and re-layouts, add_term(): left_pos[index]  14.5 us
    dot_general x1, matrix products, body(): jnp.dot(marks, piece.reshape(rows, width * width), preferred_element_type...  8.13 us
  transfers between devices with their start and end apart: 4, of which 4 were waited for; matrix products, arithmetic and copies ran while one was open for 1% of the time, Pallas kernels for 0%

commit v1 on v0

v1 whole, which is shorter than its diff:
```python
import jax
import jax.numpy as jnp
from jax import lax
from jax.experimental import pallas as pl
from jax.experimental.pallas import tpu as pltpu
from jax.sharding import PartitionSpec as P

NX, NY, NZ, NC = 4, 4, 16, 2
TILES = NY * NZ * NC
W = 128
PAUX = 32
FAR = (0, 5, -5)
NEAR = (1, -1, 2, -2)
CHUNKS = 8
PSTEP = 4
HEAD = 80
BF16, F32 = jnp.bfloat16, jnp.float32


def remote(src, dst, send, recv, device):
    return pltpu.make_async_remote_copy(
        src_ref=src,
        dst_ref=dst,
        send_sem=send,
        recv_sem=recv,
        device_id=device,
        device_id_type=pl.DeviceIdType.MESH,
    )


def kernel(
    fac, amp, lstep, rstep, own, slot, out,
    amp_v, idx_v, code, pack, marks, wide, spread, tiles, picked, landed, amat, fcat, part, parts,
    loc, s1s, s1r, ms, mr, s2s, s2r, cs, cr, s4s, s4r, fs, fr, rs, rr,
):
    t = lax.axis_index("tile")
    x = lax.axis_index("fit")
    c = lax.rem(t, NC)
    z = lax.rem(t // NC, NZ)
    y = t // (NC * NZ)

    def at(dx, dy, dz, dc):
        yy, zz = lax.rem(y + dy + NY, NY), lax.rem(z + dz + NZ, NZ)
        return ((yy * NZ + zz) * NC + lax.rem(c + dc, NC), lax.rem(x + dx, NX))

    before = (lax.rem(t + TILES - 1, TILES), x)
    after = (lax.rem(t + 1, TILES), x)
    cross = jnp.where(c == 0, before[0], after[0])

    loads = [pltpu.make_async_copy(amp, amp_v, loc.at[0])]
    for i, ref in enumerate((lstep, rstep, own, slot)):
        loads.append(pltpu.make_async_copy(ref, idx_v.at[i], loc.at[1 + i]))
    keep = pltpu.make_async_copy(fac, fcat.at[:, pl.ds(W, W)], loc.at[5])
    for copy in loads:
        copy.start()
    keep.start()

    barrier = pltpu.get_barrier_semaphore()
    peers = []
    for dy in range(NY):
        for dz in FAR:
            if dy or dz:
                peers.append(at(0, dy, dz, 0))
    for dz in (1, -1, 2, -2, 3, -3):
        peers.append(at(0, 0, dz, 0))
    peers.append(at(0, 0, 0, 1))
    for dx in range(1, NX):
        for dy in range(NY):
            peers.append(at(dx, dy, 0, 0))
    peers.append((cross, x))
    for peer in peers:
        pl.semaphore_signal(barrier, inc=1, device_id=peer, device_id_type=pl.DeviceIdType.MESH)

    for copy in loads:
        copy.wait()

    rows = amp_v[:, pl.ds(pl.multiple_of(x * 32, 32), 32), :].astype(F32).reshape(2, NY, 8, W)
    for dest in range(NY):
        pack[dest] = rows[:, dest].reshape(16, W).astype(BF16)

    lpos = jnp.clip(t + idx_v[0], 0, TILES - 1) - t + 1
    rpos = jnp.clip(t + idx_v[1], 0, TILES - 1) - t + 1
    owner = idx_v[2]
    tile = (((owner & 1) * NZ + ((owner >> 1) & (NZ - 1))) * NY + (owner >> 5)) * 2 + idx_v[3]
    terms = lpos.shape[1]
    code[...] = jnp.full(code.shape, -1, jnp.int32)
    code[0, 0:2, 0:terms] = lpos * 3 + rpos
    code[1, 0:2, 0:terms] = tile
    for s in range(2):
        block_of = (lax.broadcasted_iota(jnp.int32, (16, W), 0) == code[0, s : s + 1, :]).astype(BF16)
        tile_of = (lax.broadcasted_iota(jnp.int32, (256, W), 0) == code[1, s : s + 1, :]).astype(BF16)
        both = lax.dot_general(block_of, tile_of, (((1,), (1,)), ((), ())), preferred_element_type=F32)
        marks[y, 16 * s : 16 * (s + 1), :] = both.astype(BF16)
    spread[...] = (
        lax.broadcasted_iota(jnp.int32, (256, 2048), 1) // 8 == lax.broadcasted_iota(jnp.int32, (256, 2048), 0)
    ).astype(BF16)

    pl.semaphore_wait(barrier, len(peers))

    sent = []
    first = {}
    for dz in (5, -5, 0):
        for dy in range(NY):
            j = FAR.index(dz) * NY + dy
            dst = lax.rem(y + dy, NY)
            if dy or dz:
                first[dz, dy] = remote(pack.at[dst], tiles.at[c, z, y], s1s.at[j], s1r.at[j], at(0, dy, dz, 0))
                first[dz, dy].start()
                sent.append(first[dz, dy])
            else:
                mine = pltpu.make_async_copy(pack.at[dst], tiles.at[c, z, y], loc.at[6])
                mine.start()
    for dy in range(1, NY):
        copy = remote(marks.at[y], marks.at[y], ms.at[dy], mr.at[dy], at(0, dy, 0, 0))
        copy.start()
        sent.append(copy)

    def arrived(dz, dy):
        j = FAR.index(dz) * NY + dy
        zz, yy = lax.rem(z - dz + NZ, NZ), lax.rem(y - dy + NY, NY)
        here = tiles.at[c, zz, yy]
        remote(here, here, s1s.at[j], s1r.at[j], after).wait_recv()

    def tile_block(dz):
        return tiles.at[c, lax.rem(z - dz + 2 * NZ, NZ)]

    partner = at(0, 0, 0, 1)

    def share(dz):
        j = dz + 7
        copy = remote(tile_block(dz), tile_block(dz), cs.at[j], cr.at[j], partner)
        copy.start()
        sent.append(copy)

    near = []
    for i, dz in enumerate(FAR):
        for dy in range(NY):
            if dy or dz:
                arrived(dz, dy)
        if dz == 0:
            mine.wait()
        steps = NEAR + ((3,) if dz == 5 else ())
        for k, step in enumerate(steps):
            j = i * 5 + k
            copy = remote(tile_block(dz), tile_block(dz), s2s.at[j], s2r.at[j], at(0, 0, step, 0))
            copy.start()
            sent.append(copy)
            near.append((j, dz + step))
        share(dz)

    for dy in range(1, NY):
        here = marks.at[lax.rem(y - dy + NY, NY)]
        remote(here, here, ms.at[dy], mr.at[dy], after).wait_recv()
    row = lax.broadcasted_iota(jnp.int32, (144, 32), 0) // 8
    col = lax.broadcasted_iota(jnp.int32, (144, 32), 1)
    rowpick = (jnp.where(row >= 9, row + 7, row) == col).astype(BF16)
    same = (lax.broadcasted_iota(jnp.int32, (144, 2048), 0) & 7) == (
        lax.broadcasted_iota(jnp.int32, (144, 2048), 1) & 7
    )
    for dest in range(NY):
        blocks = jnp.dot(rowpick, marks[dest], preferred_element_type=F32).astype(BF16)
        full = jnp.dot(blocks, spread[...], preferred_element_type=F32)
        wide[dest] = jnp.where(same, full, 0.0).astype(BF16)

    for j, dz in near:
        remote(tile_block(dz), tile_block(dz), s2s.at[j], s2r.at[j], after).wait_recv()
        share(dz)
    for dz in range(-7, 9):
        here = tiles.at[1 - c, lax.rem(z - dz + 2 * NZ, NZ)]
        remote(here, here, cs.at[dz + 7], cr.at[dz + 7], after).wait_recv()

    gathered = tiles[...].reshape(2048, W)
    picked[...] = (
        jnp.dot(wide[...].reshape(NY * 144, 2048), gathered, preferred_element_type=F32)
        .astype(BF16)
        .reshape(NY, 144, W)
    )

    def part_of(ref, half):
        return ref.at[pl.ds(0, HEAD)] if half == 0 else ref.at[pl.ds(HEAD, 144 - HEAD)]

    place = x * NY + y
    for half in range(2):
        for dx in range(NX):
            for dy in range(NY):
                dst = lax.rem(y + dy, NY)
                src_ref, dst_ref = part_of(picked.at[dst], half), part_of(landed.at[place], half)
                j = dx * NY + dy
                if dx or dy:
                    copy = remote(src_ref, dst_ref, s4s.at[half, j], s4r.at[half, j], at(dx, dy, 0, 0))
                    sent.append(copy)
                else:
                    copy = pltpu.make_async_copy(src_ref, dst_ref, s4s.at[half, 0])
                copy.start()

    count = PAUX * W // CHUNKS
    for i in range(CHUNKS):
        part_rows = pl.ds(i * count, count)
        for k, (device, lane) in enumerate(((after, 0), (before, 2 * W))):
            copy = remote(fac.at[part_rows], fcat.at[part_rows, pl.ds(lane, W)], fs.at[k, i], fr.at[k, i], device)
            copy.start()
            sent.append(copy)

    def landed_half(half):
        pltpu.make_async_copy(
            part_of(picked.at[y], half), part_of(landed.at[place], half), s4s.at[half, 0]
        ).wait()
        for dx in range(NX):
            for dy in range(NY):
                if dx or dy:
                    j = dx * NY + dy
                    src = lax.rem(x - dx + NX, NX) * NY + lax.rem(y - dy + NY, NY)
                    here = part_of(landed.at[src], half)
                    remote(here, here, s4s.at[half, j], s4r.at[half, j], after).wait_recv()

    def build(s):
        for b in range(9):
            j = s * 9 + b
            lo = (j // 2) * 16
            both = landed[:, lo : lo + 16, :].astype(F32)
            block = both[:, (j % 2) * 8 : (j % 2) * 8 + 8, :].reshape(W, W).astype(BF16)
            amat[s, pl.ds((b // 3) * W, W), pl.ds((b % 3) * W, W)] = block

    sums = []
    for s in range(2):
        landed_half(s)
        build(s)
        if s == 0:
            keep.wait()
        part[s] = jnp.zeros((W, W), F32)
        for i in range(CHUNKS):
            if s == 0:
                part_rows = pl.ds(i * count, count)
                for k, lane in enumerate((0, 2 * W)):
                    here = fcat.at[part_rows, pl.ds(lane, W)]
                    remote(fac.at[part_rows], here, fs.at[k, i], fr.at[k, i], after).wait_recv()

            @pl.loop(0, count // (PSTEP * W))
            def _(q):
                start = pl.multiple_of(i * count + q * PSTEP * W, PSTEP * W)
                block = fcat[pl.ds(start, PSTEP * W), :]
                half = jnp.dot(block, amat[s], preferred_element_type=F32).astype(BF16)
                total = part[s]
                for p in range(PSTEP):
                    total += lax.dot_general(
                        half[p * W : (p + 1) * W],
                        block[p * W : (p + 1) * W],
                        (((1,), (1,)), ((), ())),
                        preferred_element_type=F32,
                    )
                part[s] = total

        for dx in range(1, NX):
            dst = lax.rem(x + dx, NX)
            copy = remote(
                part.at[s, pl.ds(pl.multiple_of(dst * 32, 32), 32)],
                parts.at[s, dx],
                rs.at[s, dx],
                rr.at[s, dx],
                at(dx, 0, 0, 0),
            )
            copy.start()
            sent.append(copy)
    for s in range(2):
        total = part[s, pl.ds(pl.multiple_of(x * 32, 32), 32), :]
        for dx in range(1, NX):
            here = parts.at[s, dx]
            remote(here, here, rs.at[s, dx], rr.at[s, dx], after).wait_recv()
            total += parts[s, dx]
        out[s] = total.astype(BF16)
    for copy in sent:
        copy.wait_send()


def body(factors, amplitudes, left_step, right_step, amp_owner, amp_slot):
    dma, any_space = pltpu.SemaphoreType.DMA, pl.BlockSpec(memory_space=pl.ANY)
    terms = left_step.shape[1]
    return pl.pallas_call(
        kernel,
        out_shape=jax.ShapeDtypeStruct((2, 32, W), BF16),
        in_specs=[any_space] * 6,
        out_specs=pl.BlockSpec(memory_space=pltpu.VMEM),
        scratch_shapes=[
            pltpu.VMEM((2, W, W), BF16),
            pltpu.VMEM((4, 2, terms), jnp.int32),
            pltpu.VMEM((2, 8, W), jnp.int32),
            pltpu.VMEM((NY, 16, W), BF16),
            pltpu.VMEM((NY, 32, 256), BF16),
            pltpu.VMEM((NY, 144, 2048), BF16),
            pltpu.VMEM((256, 2048), BF16),
            pltpu.VMEM((NC, NZ, NY, 16, W), BF16),
            pltpu.VMEM((NY, 144, W), BF16),
            pltpu.VMEM((NX * NY, 144, W), BF16),
            pltpu.VMEM((2, 3 * W, 3 * W), BF16),
            pltpu.VMEM((PAUX * W, 3 * W), BF16),
            pltpu.VMEM((2, W, W), F32),
            pltpu.VMEM((2, NX, 32, W), F32),
            dma((8,)),
            dma((12,)), dma((12,)),
            dma((4,)), dma((4,)),
            dma((15,)), dma((15,)),
            dma((16,)), dma((16,)),
            dma((2, 16)), dma((2, 16)),
            dma((2, CHUNKS)), dma((2, CHUNKS)),
            dma((2, 4)), dma((2, 4)),
        ],
        compiler_params=pltpu.CompilerParams(
            collective_id=0, has_side_effects=True, vmem_limit_bytes=56 * 2**20
        ),
        cost_estimate=pl.CostEstimate(flops=4 * 10**9, bytes_accessed=4 * 2**20, transcendentals=0),
    )(factors.reshape(PAUX * W, W), amplitudes, left_step, right_step, amp_owner, amp_slot)


def solution(mesh):
    return jax.shard_map(
        body,
        mesh=mesh,
        in_specs=(
            P("tile", "fit", None, None),
            P("tile", None, None),
            P("tile", None),
            P("tile", None),
            P("tile", None),
            P("tile", None),
        ),
        out_specs=P("tile", "fit", None),
        check_vma=False,
    )
```

time: 394 us -> 66.9 us (0.17); the launches traced: 389 us -> 66.7 us
  waiting for transfers between devices: 162 us -> 0 us
  loops' own time: 87.2 us -> 0 us
  Pallas kernels: 0 us -> 65.4 us
  matrix products: 60.7 us -> 0 us
  local copies, waits for them, and re-layouts: 32.2 us -> 1.32 us
  other arithmetic: 22.7 us -> 0 us
  between operations: 13.5 us -> 0.01 us
  starting transfers between devices: 10.2 us -> 0 us
    all_gather x1 -> x0, waiting for transfers between devices: 132 us -> none  [body(): piece = lax.all_gather(amplitudes, 'tile', axis=0, tiled=True)]
    another operation x1 -> x0, loops' own time: 87.2 us -> none  [body(): lax.fori_loop(0, count, add_term, jnp.zeros((nz_dev, width, width), jnp.f...]
    pallas_call x0 -> x1, Pallas kernels: none -> 65.4 us  [body(): pl.pallas_call(kernel, out_shape=jax.ShapeDtypeStruct((2, 32, W), BF16),...]
    dot_general x27 -> x0, matrix products: 60.7 us -> none  [the longest x26 52.5 us: add_term(): jnp.einsum('pac,pcb->ab', left_fac, half, preferred_element_type=jnp.floa...]
    dynamic_slice x52 -> x0, local copies, waits for them, and re-layouts: 29.1 us -> none  [the longest x26 14.6 us: add_term(): right_pos[index]]
    reduce_scatter x1 -> x0, waiting for transfers between devices: 20.6 us -> none  [body(): lax.psum_scatter(partial_sums, 'fit', scatter_dimension=1, tiled=True)]
    another operation x26 -> x0, other arithmetic: 17.7 us -> none
    ppermute x2 -> x0, starting transfers between devices: 10.1 us -> none  [the longest x1 5.21 us: padded(): lax.ppermute(head, axis, [((i + 1) % count, i) for i in range(ends)])]
  transfers between devices with their start and end apart: 4 -> 0, of which waited for: 4 -> 0; matrix products, arithmetic and copies ran while one was open for 1% -> 0% of each run, Pallas kernels for 0% -> 0%
where the time goes in v1:
time: 66.9 us; the launch traced here: 66.7 us
  Pallas kernels  65.4 us (98%)
  local copies, waits for them, and re-layouts  1.32 us (2%)
    pallas_call x1, Pallas kernels, body(): pl.pallas_call(kernel, out_shape=jax.ShapeDtypeStruct((2, 32, W), BF16),...  65.4 us

profile of v1, /device:TPU:1, one launch (start us, length us, event | category | flops | bytes accessed | tf_op | source)
XLA Modules:
  0.0 66.7 jit_solution(1933404115507689236)
XLA Ops:
  0.0 65.4 %shard_map.64 = bf16[2,32,128]{2,1,0:T(8,128)(2,1)} custom-call(bf16[4096,128]{1,0:T(8,128)(2,1)} %bitcast.1, bf16[2,128,128]{2,1,0:T(8,128)(2,1)} %amp.1, s32[2,13]{1,0:T(2,128)} %lstep.1, s32[2,13]{1,0:T(2,128)} %rstep.1, s32[2,13]{1,0:T(2,128)} %own.1, s32[2,13]{1,0:T(2,128)} %slot.1), custom_call_target="tpu_custom_call" | custom-call | flops 4000000000 | bytes 4194304 | tf_op jit(solution)/shard_map/pallas_call | solution.py:278
  65.4 1.3 %copy.8 = bf16[2,32,128]{2,1,0:T(8,128)(2,1)} copy(bf16[2,32,128]{2,1,0:T(8,128)(2,1)} %shard_map.64) | data formatting | bytes 32768

commit v2 on v1

v2 whole, which is shorter than its diff:
```python
import jax
import jax.numpy as jnp
from jax import lax
from jax.experimental import pallas as pl
from jax.experimental.pallas import tpu as pltpu
from jax.sharding import PartitionSpec as P

NX, NY, NZ, NC = 4, 4, 16, 2
TILES = NY * NZ * NC
W = 128
PAUX = 32
FAR = (0, 5, -5)
NEAR = (1, -1, 2, -2)
CHUNKS = 4
HEAD = 80
EARLY = 1
RELAYED = 2
BF16, F32 = jnp.bfloat16, jnp.float32


def remote(src, dst, send, recv, device):
    return pltpu.make_async_remote_copy(
        src_ref=src,
        dst_ref=dst,
        send_sem=send,
        recv_sem=recv,
        device_id=device,
        device_id_type=pl.DeviceIdType.MESH,
    )


def kernel(
    fac, amp, lstep, rstep, own, slot, out,
    amp_v, idx_v, code, pack, marks, wide, spread, tiles, picked, landed, amat, fcat, part, parts, halves, via,
    loc, s1s, s1r, ms, mr, s2s, s2r, cs, cr, s4s, s4r, fs, fr, rs, rr, vs, vr, ws,
):
    t = lax.axis_index("tile")
    x = lax.axis_index("fit")
    c = lax.rem(t, NC)
    z = lax.rem(t // NC, NZ)
    y = t // (NC * NZ)

    def at(dx, dy, dz, dc):
        yy, zz = lax.rem(y + dy + NY, NY), lax.rem(z + dz + NZ, NZ)
        return ((yy * NZ + zz) * NC + lax.rem(c + dc, NC), lax.rem(x + dx, NX))

    before = (lax.rem(t + TILES - 1, TILES), x)
    after = (lax.rem(t + 1, TILES), x)
    cross = jnp.where(c == 0, before[0], after[0])
    ends = ((z == 0) & (c == 0)) | ((z == NZ - 1) & (c == 1))
    corner = (y * NZ * NC + jnp.where(c == 0, NZ * NC - 1, 0), x)
    direct = (jnp.logical_not(ends & (c == 1)), jnp.logical_not(ends & (c == 0)))

    barrier = pltpu.get_barrier_semaphore()
    peers = []
    for dz in (5, -5, 0):
        for dy in range(NY):
            if dy or dz:
                peers.append(at(0, dy, dz, 0))
    for dz in (1, -1, 2, -2, 3, -3):
        peers.append(at(0, 0, dz, 0))
    peers.append(at(0, 0, 0, 1))
    for dx in range(1, NX):
        for dy in range(NY):
            peers.append(at(dx, dy, 0, 0))
    peers.append((cross, x))
    for peer in peers:
        pl.semaphore_signal(barrier, inc=1, device_id=peer, device_id_type=pl.DeviceIdType.MESH)

    @pl.when(ends)
    def _():
        pl.semaphore_signal(barrier, inc=1, device_id=corner, device_id_type=pl.DeviceIdType.MESH)


    loads = [pltpu.make_async_copy(amp, amp_v, loc.at[0])]
    for i, ref in enumerate((lstep, rstep, own, slot)):
        loads.append(pltpu.make_async_copy(ref, idx_v.at[i], loc.at[1 + i]))
    keep = pltpu.make_async_copy(fac, fcat.at[:, pl.ds(W, W)], loc.at[5])
    for copy in loads:
        copy.start()
    keep.start()

    for copy in loads:
        copy.wait()

    rows = amp_v[:, pl.ds(pl.multiple_of(x * 32, 32), 32), :].astype(F32).reshape(2, NY, 8, W)
    for dest in range(NY):
        pack[dest] = rows[:, dest].reshape(16, W).astype(BF16)

    lpos = jnp.clip(t + idx_v[0], 0, TILES - 1) - t + 1
    rpos = jnp.clip(t + idx_v[1], 0, TILES - 1) - t + 1
    owner = idx_v[2]
    tile = ((((owner & 1) ^ c) * NZ + ((owner >> 1) & (NZ - 1))) * NY + (owner >> 5)) * 2 + idx_v[3]
    terms = lpos.shape[1]
    code[...] = jnp.full(code.shape, -1, jnp.int32)
    code[0, 0:2, 0:terms] = lpos * 3 + rpos
    code[1, 0:2, 0:terms] = tile
    for s in range(2):
        block_of = (lax.broadcasted_iota(jnp.int32, (16, W), 0) == code[0, s : s + 1, :]).astype(BF16)
        tile_of = (lax.broadcasted_iota(jnp.int32, (256, W), 0) == code[1, s : s + 1, :]).astype(BF16)
        both = lax.dot_general(block_of, tile_of, (((1,), (1,)), ((), ())), preferred_element_type=F32)
        marks[y, 16 * s : 16 * (s + 1), :] = both.astype(BF16)
    pl.semaphore_wait(barrier, len(peers) + jnp.where(ends, 1, 0))

    count = PAUX * W // CHUNKS

    def factor_copy(i, k):
        part_rows = pl.ds(i * count, count)
        device, lane = ((after, 0), (before, 2 * W))[k]
        return remote(fac.at[part_rows], fcat.at[part_rows, pl.ds(lane, W)], fs.at[k, i], fr.at[k, i], device)

    def start_factors(lo, hi):
        for i in range(lo, hi):
            for k in range(2):
                copy = factor_copy(i, k)
                if i < RELAYED:
                    copy.start()
                    sent.append(copy)
                else:
                    pl.when(direct[k])(copy.start)

    def relay_copy(i):
        dy = jnp.where(c == 1, 1, -1)
        return remote(
            fac.at[pl.ds(i * count, count)], via.at[i - RELAYED], vs.at[i - RELAYED], vr.at[i - RELAYED], at(0, dy, 0, 0)
        )

    def relay_on(i, k):
        dst = fcat.at[pl.ds(i * count, count), pl.ds(2 * W * k, W)]
        return remote(via.at[i - RELAYED], dst, ws.at[i - RELAYED], fr.at[k, i], corner)

    sent = []
    first = {}
    for dz in (5, -5, 0):
        for dy in range(NY):
            j = FAR.index(dz) * NY + dy
            dst = lax.rem(y + dy, NY)
            if dy or dz:
                first[dz, dy] = remote(pack.at[dst], tiles.at[0, z, y], s1s.at[j], s1r.at[j], at(0, dy, dz, 0))
                first[dz, dy].start()
                sent.append(first[dz, dy])
            else:
                mine = pltpu.make_async_copy(pack.at[dst], tiles.at[0, z, y], loc.at[6])
                mine.start()
    for dy in range(1, NY):
        copy = remote(marks.at[y], marks.at[y], ms.at[dy], mr.at[dy], at(0, dy, 0, 0))
        copy.start()
        sent.append(copy)

    spread[...] = (
        lax.broadcasted_iota(jnp.int32, (256, 2048), 1) // 8 == lax.broadcasted_iota(jnp.int32, (256, 2048), 0)
    ).astype(BF16)

    start_factors(0, EARLY)

    @pl.when(ends)
    def _():
        for i in range(RELAYED, CHUNKS):
            relay_copy(i).start()


    def arrived(dz, dy):
        j = FAR.index(dz) * NY + dy
        zz, yy = lax.rem(z - dz + NZ, NZ), lax.rem(y - dy + NY, NY)
        here = tiles.at[0, zz, yy]
        remote(here, here, s1s.at[j], s1r.at[j], after).wait_recv()

    def tile_block(dz, core=0):
        return tiles.at[core, lax.rem(z - dz + 2 * NZ, NZ)]

    partner = at(0, 0, 0, 1)

    def share(dz):
        j = dz + 7
        copy = remote(tile_block(dz), tile_block(dz, 1), cs.at[j], cr.at[j], partner)
        copy.start()
        sent.append(copy)

    near = []
    for i, dz in enumerate(FAR):
        for dy in range(NY):
            if dy or dz:
                arrived(dz, dy)
        if dz == 0:
            mine.wait()
        steps = NEAR + ((3,) if dz == 5 else ())
        for k, step in enumerate(steps):
            j = i * 5 + k
            copy = remote(tile_block(dz), tile_block(dz), s2s.at[j], s2r.at[j], at(0, 0, step, 0))
            copy.start()
            sent.append(copy)
            near.append((j, dz + step))
        share(dz)

    start_factors(EARLY, CHUNKS)
    for dy in range(1, NY):
        here = marks.at[lax.rem(y - dy + NY, NY)]
        remote(here, here, ms.at[dy], mr.at[dy], after).wait_recv()
    row = lax.broadcasted_iota(jnp.int32, (144, 32), 0) // 8
    col = lax.broadcasted_iota(jnp.int32, (144, 32), 1)
    rowpick = (jnp.where(row >= 9, row + 7, row) == col).astype(BF16)
    same = (lax.broadcasted_iota(jnp.int32, (144, 2048), 0) & 7) == (
        lax.broadcasted_iota(jnp.int32, (144, 2048), 1) & 7
    )
    for dest in range(NY):
        blocks = jnp.dot(rowpick, marks[dest], preferred_element_type=F32).astype(BF16)
        full = jnp.dot(blocks, spread[...], preferred_element_type=F32)
        wide[dest] = jnp.where(same, full, 0.0).astype(BF16)

    for j, dz in near:
        remote(tile_block(dz), tile_block(dz), s2s.at[j], s2r.at[j], after).wait_recv()
        share(dz)

    @pl.when(ends)
    def _():
        for i in range(RELAYED, CHUNKS):
            relay_copy(i).wait_recv()
            for k in range(2):
                pl.when(c == 1 - k)(relay_on(i, k).start)

    own_half = jnp.dot(
        wide[:, :, :1024].reshape(NY * 144, 1024), tiles[0].reshape(1024, W), preferred_element_type=F32
    )
    for dz in range(-7, 9):
        here = tile_block(dz, 1)
        remote(here, here, cs.at[dz + 7], cr.at[dz + 7], after).wait_recv()
    other_half = jnp.dot(
        wide[:, :, 1024:].reshape(NY * 144, 1024), tiles[1].reshape(1024, W), preferred_element_type=F32
    )
    picked[...] = (own_half + other_half).astype(BF16).reshape(NY, 144, W)

    place = x * NY + y

    def half_of(ref, s):
        return ref.at[pl.ds(0, HEAD)] if s == 0 else ref.at[pl.ds(HEAD, 144 - HEAD)]

    kept = []
    for s in range(2):
        for dx in range(NX):
            for dy in range(NY):
                src_ref, dst_ref = half_of(picked.at[lax.rem(y + dy, NY)], s), half_of(landed.at[place], s)
                j = dx * NY + dy
                if dx or dy:
                    copy = remote(src_ref, dst_ref, s4s.at[s, j], s4r.at[s, j], at(dx, dy, 0, 0))
                    sent.append(copy)
                else:
                    copy = pltpu.make_async_copy(src_ref, dst_ref, s4s.at[s, 0])
                    kept.append(copy)
                copy.start()

    def blocks_here(s):
        kept[s].wait()
        for dx in range(NX):
            for dy in range(NY):
                if dx or dy:
                    j = dx * NY + dy
                    here = half_of(landed.at[lax.rem(x - dx + NX, NX) * NY + lax.rem(y - dy + NY, NY)], s)
                    remote(here, here, s4s.at[s, j], s4r.at[s, j], after).wait_recv()
        for b in range(9):
            j = s * 9 + b
            both = landed[:, (j // 2) * 16 : (j // 2) * 16 + 16, :].astype(F32)
            block = both[:, (j % 2) * 8 : (j % 2) * 8 + 8, :].reshape(W, W).astype(BF16)
            amat[s, pl.ds((b // 3) * W, W), pl.ds((b % 3) * W, W)] = block

    def factors_here(i):
        for k, lane in enumerate((0, 2 * W)):
            here = fcat.at[pl.ds(i * count, count), pl.ds(lane, W)]
            remote(fac.at[pl.ds(i * count, count)], here, fs.at[k, i], fr.at[k, i], after).wait_recv()

    def right_products(i, s):
        halves[i % 2] = jnp.dot(fcat[pl.ds(i * count, count), :], amat[s], preferred_element_type=F32).astype(BF16)

    def left_products(i, s):
        half, block = halves[i % 2], fcat[pl.ds(i * count, count), :]
        steps = range(0, count, W)
        right = jnp.concatenate([block[p : p + W] for p in steps], axis=1)
        left = jnp.concatenate([half[p : p + W] for p in steps], axis=1)
        term = lax.dot_general(left, right, (((1,), (1,)), ((), ())), preferred_element_type=F32)
        part[s] = term if i == 0 else part[s] + term

    def reduce_start(s):
        for dx in range(1, NX):
            rows = pl.ds(pl.multiple_of(lax.rem(x + dx, NX) * 32, 32), 32)
            copy = remote(part.at[s, rows], parts.at[dx, s], rs.at[s, dx], rr.at[s, dx], at(dx, 0, 0, 0))
            copy.start()
            sent.append(copy)

    keep.wait()
    for s in range(2):
        blocks_here(s)
        for i in range(CHUNKS):
            if s == 0:
                factors_here(i)
            right_products(i, s)
            if i:
                left_products(i - 1, s)
        left_products(CHUNKS - 1, s)
        reduce_start(s)
    total = part[:, pl.ds(pl.multiple_of(x * 32, 32), 32), :]
    for dx in range(1, NX):
        for s in range(2):
            here = parts.at[dx, s]
            remote(here, here, rs.at[s, dx], rr.at[s, dx], after).wait_recv()
        total += parts[dx]
    out[...] = total.astype(BF16)
    for copy in sent:
        copy.wait_send()
    for i in range(RELAYED, CHUNKS):
        for k in range(2):
            pl.when(direct[k])(factor_copy(i, k).wait_send)

    @pl.when(ends)
    def _():
        for i in range(RELAYED, CHUNKS):
            relay_copy(i).wait_send()
            relay_on(i, 0).wait_send()


def body(factors, amplitudes, left_step, right_step, amp_owner, amp_slot):
    dma, any_space = pltpu.SemaphoreType.DMA, pl.BlockSpec(memory_space=pl.ANY)
    terms = left_step.shape[1]
    return pl.pallas_call(
        kernel,
        out_shape=jax.ShapeDtypeStruct((2, 32, W), BF16),
        in_specs=[any_space] * 6,
        out_specs=pl.BlockSpec(memory_space=pltpu.VMEM),
        scratch_shapes=[
            pltpu.VMEM((2, W, W), BF16),
            pltpu.VMEM((4, 2, terms), jnp.int32),
            pltpu.VMEM((2, 8, W), jnp.int32),
            pltpu.VMEM((NY, 16, W), BF16),
            pltpu.VMEM((NY, 32, 256), BF16),
            pltpu.VMEM((NY, 144, 2048), BF16),
            pltpu.VMEM((256, 2048), BF16),
            pltpu.VMEM((NC, NZ, NY, 16, W), BF16),
            pltpu.VMEM((NY, 144, W), BF16),
            pltpu.VMEM((NX * NY, 144, W), BF16),
            pltpu.VMEM((2, 3 * W, 3 * W), BF16),
            pltpu.VMEM((PAUX * W, 3 * W), BF16),
            pltpu.VMEM((2, W, W), F32),
            pltpu.VMEM((NX, 2, 32, W), F32),
            pltpu.VMEM((2, PAUX * W // CHUNKS, 3 * W), BF16),
            pltpu.VMEM((CHUNKS - RELAYED, PAUX * W // CHUNKS, W), BF16),
            dma((8,)),
            dma((12,)), dma((12,)),
            dma((4,)), dma((4,)),
            dma((15,)), dma((15,)),
            dma((16,)), dma((16,)),
            dma((2, 16)), dma((2, 16)),
            dma((2, CHUNKS)), dma((2, CHUNKS)),
            dma((2, 4)), dma((2, 4)),
            dma((CHUNKS - RELAYED,)), dma((CHUNKS - RELAYED,)), dma((CHUNKS - RELAYED,)),
        ],
        compiler_params=pltpu.CompilerParams(
            collective_id=0, has_side_effects=True, vmem_limit_bytes=56 * 2**20
        ),
        cost_estimate=pl.CostEstimate(flops=4 * 10**9, bytes_accessed=4 * 2**20, transcendentals=0),
    )(factors.reshape(PAUX * W, W), amplitudes, left_step, right_step, amp_owner, amp_slot)


def solution(mesh):
    return jax.shard_map(
        body,
        mesh=mesh,
        in_specs=(
            P("tile", "fit", None, None),
            P("tile", None, None),
            P("tile", None),
            P("tile", None),
            P("tile", None),
            P("tile", None),
        ),
        out_specs=P("tile", "fit", None),
        check_vma=False,
    )
```

time: 66.9 us -> 52.7 us (0.79)
  Pallas kernels: 65.4 us -> 51.1 us
    pallas_call x1, Pallas kernels: 65.4 us -> 51.1 us  [body(): pl.pallas_call(kernel, out_shape=jax.ShapeDtypeStruct((2, 32, W), BF16),...]
where the time goes in v2:
time: 52.7 us; the launch traced here: 52.5 us
  Pallas kernels  51.1 us (97%)
  local copies, waits for them, and re-layouts  1.32 us (3%)
    pallas_call x1, Pallas kernels, body(): pl.pallas_call(kernel, out_shape=jax.ShapeDtypeStruct((2, 32, W), BF16),...  51.1 us
    unnamed x1, local copies, waits for them, and re-layouts  1.32 us

profile of v2, /device:TPU:1, one launch (start us, length us, event | category | flops | bytes accessed | tf_op | source)
XLA Modules:
  0.0 52.5 jit_solution(15562470096493420017)
XLA Ops:
  0.0 51.1 %shard_map.64 = bf16[2,32,128]{2,1,0:T(8,128)(2,1)} custom-call(bf16[4096,128]{1,0:T(8,128)(2,1)} %bitcast.1, bf16[2,128,128]{2,1,0:T(8,128)(2,1)} %amp.1, s32[2,13]{1,0:T(2,128)} %lstep.1, s32[2,13]{1,0:T(2,128)} %rstep.1, s32[2,13]{1,0:T(2,128)} %own.1, s32[2,13]{1,0:T(2,128)} %slot.1), custom_call_target="tpu_custom_call" | custom-call | flops 4000000000 | bytes 4194304 | tf_op jit(solution)/shard_map/pallas_call | solution.py:322
  51.1 1.3 %copy.8 = bf16[2,32,128]{2,1,0:T(8,128)(2,1)} copy(bf16[2,32,128]{2,1,0:T(8,128)(2,1)} %shard_map.64) | data formatting | bytes 32768

commit v3 on v2

--- a/solution.py
+++ b/solution.py
@@ -12,7 +12,8 @@
 FAR = (0, 5, -5)
 NEAR = (1, -1, 2, -2)
 CHUNKS = 4
-HEAD = 80
+GROUP = 48
+ORDER = (1, 0, 2)
 EARLY = 1
 RELAYED = 2
 BF16, F32 = jnp.bfloat16, jnp.float32
@@ -198,7 +199,7 @@
         remote(here, here, ms.at[dy], mr.at[dy], after).wait_recv()
     row = lax.broadcasted_iota(jnp.int32, (144, 32), 0) // 8
     col = lax.broadcasted_iota(jnp.int32, (144, 32), 1)
-    rowpick = (jnp.where(row >= 9, row + 7, row) == col).astype(BF16)
+    rowpick = (row // 6 + 3 * (row % 3) + 16 * ((row // 3) & 1) == col).astype(BF16)
     same = (lax.broadcasted_iota(jnp.int32, (144, 2048), 0) & 7) == (
         lax.broadcasted_iota(jnp.int32, (144, 2048), 1) & 7
     )
@@ -218,89 +219,90 @@
             for k in range(2):
                 pl.when(c == 1 - k)(relay_on(i, k).start)
 
-    own_half = jnp.dot(
-        wide[:, :, :1024].reshape(NY * 144, 1024), tiles[0].reshape(1024, W), preferred_element_type=F32
-    )
+    def picks(g, core):
+        marked = wide[:, GROUP * g : GROUP * (g + 1), 1024 * core : 1024 * (core + 1)].reshape(NY * GROUP, 1024)
+        return jnp.dot(marked, tiles[core].reshape(1024, W), preferred_element_type=F32)
+
+    own_half = [picks(g, 0) for g in ORDER]
     for dz in range(-7, 9):
         here = tile_block(dz, 1)
         remote(here, here, cs.at[dz + 7], cr.at[dz + 7], after).wait_recv()
-    other_half = jnp.dot(
-        wide[:, :, 1024:].reshape(NY * 144, 1024), tiles[1].reshape(1024, W), preferred_element_type=F32
-    )
-    picked[...] = (own_half + other_half).astype(BF16).reshape(NY, 144, W)
-
     place = x * NY + y
 
-    def half_of(ref, s):
-        return ref.at[pl.ds(0, HEAD)] if s == 0 else ref.at[pl.ds(HEAD, 144 - HEAD)]
-
-    kept = []
-    for s in range(2):
-        for dx in range(NX):
-            for dy in range(NY):
-                src_ref, dst_ref = half_of(picked.at[lax.rem(y + dy, NY)], s), half_of(landed.at[place], s)
+    def group_of(ref, g):
+        return ref.at[pl.ds(GROUP * g, GROUP)]
+
+    kept = {}
+    for n, g in enumerate(ORDER):
+        both = (own_half[n] + picks(g, 1)).astype(BF16)
+        picked[:, GROUP * g : GROUP * (g + 1), :] = both.reshape(NY, GROUP, W)
+        for dx in (2, 1, 3, 0):
+            for dy in (2, 1, 3, 0):
+                src_ref, dst_ref = group_of(picked.at[lax.rem(y + dy, NY)], g), group_of(landed.at[place], g)
                 j = dx * NY + dy
                 if dx or dy:
-                    copy = remote(src_ref, dst_ref, s4s.at[s, j], s4r.at[s, j], at(dx, dy, 0, 0))
+                    copy = remote(src_ref, dst_ref, s4s.at[g, j], s4r.at[g, j], at(dx, dy, 0, 0))
                     sent.append(copy)
                 else:
-                    copy = pltpu.make_async_copy(src_ref, dst_ref, s4s.at[s, 0])
-                    kept.append(copy)
+                    copy = kept[g] = pltpu.make_async_copy(src_ref, dst_ref, s4s.at[g, 0])
                 copy.start()
 
-    def blocks_here(s):
-        kept[s].wait()
+    def blocks_here(g):
+        kept[g].wait()
         for dx in range(NX):
             for dy in range(NY):
                 if dx or dy:
                     j = dx * NY + dy
-                    here = half_of(landed.at[lax.rem(x - dx + NX, NX) * NY + lax.rem(y - dy + NY, NY)], s)
-                    remote(here, here, s4s.at[s, j], s4r.at[s, j], after).wait_recv()
-        for b in range(9):
-            j = s * 9 + b
-            both = landed[:, (j // 2) * 16 : (j // 2) * 16 + 16, :].astype(F32)
-            block = both[:, (j % 2) * 8 : (j % 2) * 8 + 8, :].reshape(W, W).astype(BF16)
-            amat[s, pl.ds((b // 3) * W, W), pl.ds((b % 3) * W, W)] = block
+                    here = group_of(landed.at[lax.rem(x - dx + NX, NX) * NY + lax.rem(y - dy + NY, NY)], g)
+                    remote(here, here, s4s.at[g, j], s4r.at[g, j], after).wait_recv()
+        for j in range(0, 6, 2):
+            lo = GROUP * g + 8 * j
+            both = landed[:, lo : lo + 16, :].astype(F32)
+            for k in range(2):
+                s, left = divmod(j + k, 3)
+                block = both[:, 8 * k : 8 * k + 8, :].reshape(W, W).astype(BF16)
+                amat[g, pl.ds(left * W, W), pl.ds(s * W, W)] = block
 
     def factors_here(i):
         for k, lane in enumerate((0, 2 * W)):
             here = fcat.at[pl.ds(i * count, count), pl.ds(lane, W)]
             remote(fac.at[pl.ds(i * count, count)], here, fs.at[k, i], fr.at[k, i], after).wait_recv()
 
-    def right_products(i, s):
-        halves[i % 2] = jnp.dot(fcat[pl.ds(i * count, count), :], amat[s], preferred_element_type=F32).astype(BF16)
-
-    def left_products(i, s):
-        half, block = halves[i % 2], fcat[pl.ds(i * count, count), :]
+    def right_products(i, g):
+        halves[i % 2] = jnp.dot(fcat[pl.ds(i * count, count), :], amat[g], preferred_element_type=F32).astype(BF16)
+
+    def left_products(i, g):
+        half, block = halves[i % 2], fcat[pl.ds(i * count, count), g * W : (g + 1) * W]
         steps = range(0, count, W)
         right = jnp.concatenate([block[p : p + W] for p in steps], axis=1)
-        left = jnp.concatenate([half[p : p + W] for p in steps], axis=1)
+        left = jnp.concatenate(
+            [jnp.concatenate([half[p : p + W, s * W : (s + 1) * W] for p in steps], axis=1) for s in range(2)], axis=0
+        )
         term = lax.dot_general(left, right, (((1,), (1,)), ((), ())), preferred_element_type=F32)
-        part[s] = term if i == 0 else part[s] + term
-
-    def reduce_start(s):
-        for dx in range(1, NX):
-            rows = pl.ds(pl.multiple_of(lax.rem(x + dx, NX) * 32, 32), 32)
-            copy = remote(part.at[s, rows], parts.at[dx, s], rs.at[s, dx], rr.at[s, dx], at(dx, 0, 0, 0))
-            copy.start()
-            sent.append(copy)
+        part[...] += term.reshape(2, W, W)
 
     keep.wait()
-    for s in range(2):
-        blocks_here(s)
-        for i in range(CHUNKS):
-            if s == 0:
-                factors_here(i)
-            right_products(i, s)
-            if i:
-                left_products(i - 1, s)
-        left_products(CHUNKS - 1, s)
-        reduce_start(s)
+    part[...] = jnp.zeros(part.shape, F32)
+    todo = [(i, g) for g in ORDER for i in range(CHUNKS)]
+    for n, (i, g) in enumerate(todo):
+        if i == 0:
+            blocks_here(g)
+        if g == ORDER[0]:
+            factors_here(i)
+        right_products(i, g)
+        if n:
+            left_products(*todo[n - 1])
+    left_products(*todo[-1])
+
+    for dx in (2, 1, 3):
+        rows = pl.ds(pl.multiple_of(lax.rem(x + dx, NX) * 32, 32), 32)
+        copy = remote(part.at[:, rows], parts.at[dx], rs.at[dx], rr.at[dx], at(dx, 0, 0, 0))
+        copy.start()
+        sent.append(copy)
     total = part[:, pl.ds(pl.multiple_of(x * 32, 32), 32), :]
     for dx in range(1, NX):
-        for s in range(2):
-            here = parts.at[dx, s]
-            remote(here, here, rs.at[s, dx], rr.at[s, dx], after).wait_recv()
+        here = parts.at[dx]
+        remote(here, here, rs.at[dx], rr.at[dx], after).wait_recv()
         total += parts[dx]
     out[...] = total.astype(BF16)
     for copy in sent:
@@ -335,20 +337,20 @@
             pltpu.VMEM((NC, NZ, NY, 16, W), BF16),
             pltpu.VMEM((NY, 144, W), BF16),
             pltpu.VMEM((NX * NY, 144, W), BF16),
-            pltpu.VMEM((2, 3 * W, 3 * W), BF16),
+            pltpu.VMEM((3, 3 * W, 2 * W), BF16),
             pltpu.VMEM((PAUX * W, 3 * W), BF16),
             pltpu.VMEM((2, W, W), F32),
             pltpu.VMEM((NX, 2, 32, W), F32),
-            pltpu.VMEM((2, PAUX * W // CHUNKS, 3 * W), BF16),
+            pltpu.VMEM((2, PAUX * W // CHUNKS, 2 * W), BF16),
             pltpu.VMEM((CHUNKS - RELAYED, PAUX * W // CHUNKS, W), BF16),
             dma((8,)),
             dma((12,)), dma((12,)),
             dma((4,)), dma((4,)),
             dma((15,)), dma((15,)),
             dma((16,)), dma((16,)),
-            dma((2, 16)), dma((2, 16)),
+            dma((3, 16)), dma((3, 16)),
             dma((2, CHUNKS)), dma((2, CHUNKS)),
-            dma((2, 4)), dma((2, 4)),
+            dma((4,)), dma((4,)),
             dma((CHUNKS - RELAYED,)), dma((CHUNKS - RELAYED,)), dma((CHUNKS - RELAYED,)),
         ],
         compiler_params=pltpu.CompilerParams(

time: 52.7 us -> 50.8 us (0.964)
  Pallas kernels: 51.1 us -> 49.2 us
    pallas_call x1, Pallas kernels: 51.1 us -> 49.2 us  [body(): pl.pallas_call(kernel, out_shape=jax.ShapeDtypeStruct((2, 32, W), BF16),...]
where the time goes in v3:
time: 50.8 us; the launch traced here: 50.6 us
  Pallas kernels  49.2 us (97%)
  local copies, waits for them, and re-layouts  1.32 us (3%)
    pallas_call x1, Pallas kernels, body(): pl.pallas_call(kernel, out_shape=jax.ShapeDtypeStruct((2, 32, W), BF16),...  49.2 us
    unnamed x1, local copies, waits for them, and re-layouts  1.32 us

profile of v3, /device:TPU:1, one launch (start us, length us, event | category | flops | bytes accessed | tf_op | source)
XLA Modules:
  0.0 50.6 jit_solution(16579364525654967332)
XLA Ops:
  0.0 49.2 %shard_map.64 = bf16[2,32,128]{2,1,0:T(8,128)(2,1)} custom-call(bf16[4096,128]{1,0:T(8,128)(2,1)} %bitcast.1, bf16[2,128,128]{2,1,0:T(8,128)(2,1)} %amp.1, s32[2,13]{1,0:T(2,128)} %lstep.1, s32[2,13]{1,0:T(2,128)} %rstep.1, s32[2,13]{1,0:T(2,128)} %own.1, s32[2,13]{1,0:T(2,128)} %slot.1), custom_call_target="tpu_custom_call" | custom-call | flops 4000000000 | bytes 4194304 | tf_op jit(solution)/shard_map/pallas_call | solution.py:324
  49.2 1.3 %copy.8 = bf16[2,32,128]{2,1,0:T(8,128)(2,1)} copy(bf16[2,32,128]{2,1,0:T(8,128)(2,1)} %shard_map.64) | data formatting | bytes 32768

commit v4 on v3

--- a/solution.py
+++ b/solution.py
@@ -53,17 +53,16 @@
     direct = (jnp.logical_not(ends & (c == 1)), jnp.logical_not(ends & (c == 0)))
 
     barrier = pltpu.get_barrier_semaphore()
-    peers = []
-    for dz in (5, -5, 0):
-        for dy in range(NY):
-            if dy or dz:
-                peers.append(at(0, dy, dz, 0))
-    for dz in (1, -1, 2, -2, 3, -3):
-        peers.append(at(0, 0, dz, 0))
-    peers.append(at(0, 0, 0, 1))
-    for dx in range(1, NX):
-        for dy in range(NY):
-            peers.append(at(dx, dy, 0, 0))
+    steps = {(0, 0, 0, 1)}
+    for dy in range(NY):
+        steps |= {(0, dy, dz, 0) for dz in FAR} | {(dx, dy, 0, 0) for dx in range(NX)}
+    steps |= {(0, 0, dz, 0) for dz in (1, -1, 2, -2, 3, -3)}
+    steps.discard((0, 0, 0, 0))
+
+    def hops(step):
+        return (min(step[0], NX - step[0]) + min(step[1], NY - step[1]) + abs(step[2]), step)
+
+    peers = [at(*step) for step in sorted(steps, key=hops, reverse=True)]
     peers.append((cross, x))
     for peer in peers:
         pl.semaphore_signal(barrier, inc=1, device_id=peer, device_id_type=pl.DeviceIdType.MESH)
@@ -133,7 +132,7 @@
     sent = []
     first = {}
     for dz in (5, -5, 0):
-        for dy in range(NY):
+        for dy in (2, 1, 3, 0):
             j = FAR.index(dz) * NY + dy
             dst = lax.rem(y + dy, NY)
             if dy or dz:
@@ -173,7 +172,7 @@
 
     def share(dz):
         j = dz + 7
-        copy = remote(tile_block(dz), tile_block(dz, 1), cs.at[j], cr.at[j], partner)
+        copy = remote(tile_block(dz), tile_block(dz, 1), cs.at[j], cr.at[0], partner)
         copy.start()
         sent.append(copy)
 
@@ -224,9 +223,8 @@
         return jnp.dot(marked, tiles[core].reshape(1024, W), preferred_element_type=F32)
 
     own_half = [picks(g, 0) for g in ORDER]
-    for dz in range(-7, 9):
-        here = tile_block(dz, 1)
-        remote(here, here, cs.at[dz + 7], cr.at[dz + 7], after).wait_recv()
+    remote(tiles.at[1], tiles.at[1], cs.at[0], cr.at[0], partner).wait_recv()
+
     place = x * NY + y
 
     def group_of(ref, g):
@@ -241,7 +239,7 @@
                 src_ref, dst_ref = group_of(picked.at[lax.rem(y + dy, NY)], g), group_of(landed.at[place], g)
                 j = dx * NY + dy
                 if dx or dy:
-                    copy = remote(src_ref, dst_ref, s4s.at[g, j], s4r.at[g, j], at(dx, dy, 0, 0))
+                    copy = remote(src_ref, dst_ref, s4s.at[g, j], s4r.at[g], at(dx, dy, 0, 0))
                     sent.append(copy)
                 else:
                     copy = kept[g] = pltpu.make_async_copy(src_ref, dst_ref, s4s.at[g, 0])
@@ -249,12 +247,8 @@
 
     def blocks_here(g):
         kept[g].wait()
-        for dx in range(NX):
-            for dy in range(NY):
-                if dx or dy:
-                    j = dx * NY + dy
-                    here = group_of(landed.at[lax.rem(x - dx + NX, NX) * NY + lax.rem(y - dy + NY, NY)], g)
-                    remote(here, here, s4s.at[g, j], s4r.at[g, j], after).wait_recv()
+        others = landed.at[pl.ds(0, NX * NY - 1), pl.ds(GROUP * g, GROUP)]
+        remote(others, others, s4s.at[g, 1], s4r.at[g], after).wait_recv()
         for j in range(0, 6, 2):
             lo = GROUP * g + 8 * j
             both = landed[:, lo : lo + 16, :].astype(F32)
@@ -275,11 +269,9 @@
         half, block = halves[i % 2], fcat[pl.ds(i * count, count), g * W : (g + 1) * W]
         steps = range(0, count, W)
         right = jnp.concatenate([block[p : p + W] for p in steps], axis=1)
-        left = jnp.concatenate(
-            [jnp.concatenate([half[p : p + W, s * W : (s + 1) * W] for p in steps], axis=1) for s in range(2)], axis=0
-        )
-        term = lax.dot_general(left, right, (((1,), (1,)), ((), ())), preferred_element_type=F32)
-        part[...] += term.reshape(2, W, W)
+        for s in range(2):
+            left = jnp.concatenate([half[p : p + W, s * W : (s + 1) * W] for p in steps], axis=1)
+            part[s] += lax.dot_general(left, right, (((1,), (1,)), ((), ())), preferred_element_type=F32)
 
     keep.wait()
     part[...] = jnp.zeros(part.shape, F32)
@@ -294,28 +286,32 @@
             left_products(*todo[n - 1])
     left_products(*todo[-1])
 
+    last = []
     for dx in (2, 1, 3):
         rows = pl.ds(pl.multiple_of(lax.rem(x + dx, NX) * 32, 32), 32)
         copy = remote(part.at[:, rows], parts.at[dx], rs.at[dx], rr.at[dx], at(dx, 0, 0, 0))
         copy.start()
-        sent.append(copy)
+        last.append(copy)
+    for copy in sent:
+        copy.wait_send()
+    for i in range(RELAYED, CHUNKS):
+        for k in range(2):
+            pl.when(direct[k])(factor_copy(i, k).wait_send)
+
+    @pl.when(ends)
+    def _():
+        for i in range(RELAYED, CHUNKS):
+            relay_copy(i).wait_send()
+            relay_on(i, 0).wait_send()
+
     total = part[:, pl.ds(pl.multiple_of(x * 32, 32), 32), :]
     for dx in range(1, NX):
         here = parts.at[dx]
         remote(here, here, rs.at[dx], rr.at[dx], after).wait_recv()
         total += parts[dx]
     out[...] = total.astype(BF16)
-    for copy in sent:
+    for copy in last:
         copy.wait_send()
-    for i in range(RELAYED, CHUNKS):
-        for k in range(2):
-            pl.when(direct[k])(factor_copy(i, k).wait_send)
-
-    @pl.when(ends)
-    def _():
-        for i in range(RELAYED, CHUNKS):
-            relay_copy(i).wait_send()
-            relay_on(i, 0).wait_send()
 
 
 def body(factors, amplitudes, left_step, right_step, amp_owner, amp_slot):
@@ -347,8 +343,8 @@
             dma((12,)), dma((12,)),
             dma((4,)), dma((4,)),
             dma((15,)), dma((15,)),
-            dma((16,)), dma((16,)),
-            dma((3, 16)), dma((3, 16)),
+            dma((16,)), dma((1,)),
+            dma((3, 16)), dma((3,)),
             dma((2, CHUNKS)), dma((2, CHUNKS)),
             dma((4,)), dma((4,)),
             dma((CHUNKS - RELAYED,)), dma((CHUNKS - RELAYED,)), dma((CHUNKS - RELAYED,)),

time: 50.8 us -> 49.3 us (0.970)
  Pallas kernels: 49.2 us -> 47.8 us
    pallas_call x1, Pallas kernels: 49.2 us -> 47.8 us  [body(): pl.pallas_call(kernel, out_shape=jax.ShapeDtypeStruct((2, 32, W), BF16),...]
where the time goes in v4:
time: 49.3 us; the launch traced here: 49.1 us
  Pallas kernels  47.8 us (97%)
  local copies, waits for them, and re-layouts  1.32 us (3%)
    pallas_call x1, Pallas kernels, body(): pl.pallas_call(kernel, out_shape=jax.ShapeDtypeStruct((2, 32, W), BF16),...  47.8 us
    unnamed x1, local copies, waits for them, and re-layouts  1.32 us

profile of v4, /device:TPU:1, one launch (start us, length us, event | category | flops | bytes accessed | tf_op | source)
XLA Modules:
  0.0 49.1 jit_solution(15285161141859254422)
XLA Ops:
  0.0 47.8 %shard_map.64 = bf16[2,32,128]{2,1,0:T(8,128)(2,1)} custom-call(bf16[4096,128]{1,0:T(8,128)(2,1)} %bitcast.1, bf16[2,128,128]{2,1,0:T(8,128)(2,1)} %amp.1, s32[2,13]{1,0:T(2,128)} %lstep.1, s32[2,13]{1,0:T(2,128)} %rstep.1, s32[2,13]{1,0:T(2,128)} %own.1, s32[2,13]{1,0:T(2,128)} %slot.1), custom_call_target="tpu_custom_call" | custom-call | flops 4000000000 | bytes 4194304 | tf_op jit(solution)/shard_map/pallas_call | solution.py:320
  47.8 1.3 %copy.8 = bf16[2,32,128]{2,1,0:T(8,128)(2,1)} copy(bf16[2,32,128]{2,1,0:T(8,128)(2,1)} %shard_map.64) | data formatting | bytes 32768

commit v5 on v4

--- a/solution.py
+++ b/solution.py
@@ -10,7 +10,7 @@
 W = 128
 PAUX = 32
 FAR = (0, 5, -5)
-NEAR = (1, -1, 2, -2)
+NEAR = (2, -2, 1, -1)
 CHUNKS = 4
 GROUP = 48
 ORDER = (1, 0, 2)
@@ -183,7 +183,7 @@
                 arrived(dz, dy)
         if dz == 0:
             mine.wait()
-        steps = NEAR + ((3,) if dz == 5 else ())
+        steps = ((3,) if dz == 5 else ()) + NEAR
         for k, step in enumerate(steps):
             j = i * 5 + k
             copy = remote(tile_block(dz), tile_block(dz), s2s.at[j], s2r.at[j], at(0, 0, step, 0))

time: 49.3 us -> 49.4 us (level)
  no operation moved by 1% of the time
where the time goes in v5:
time: 49.4 us; the launch traced here: 49.2 us
  Pallas kernels  47.9 us (97%)
  local copies, waits for them, and re-layouts  1.32 us (3%)
    pallas_call x1, Pallas kernels, body(): pl.pallas_call(kernel, out_shape=jax.ShapeDtypeStruct((2, 32, W), BF16),...  47.9 us
    unnamed x1, local copies, waits for them, and re-layouts  1.32 us

profile of v5, /device:TPU:1, one launch (start us, length us, event | category | flops | bytes accessed | tf_op | source)
XLA Modules:
  0.0 49.2 jit_solution(13348325453514211863)
XLA Ops:
  0.0 47.9 %shard_map.64 = bf16[2,32,128]{2,1,0:T(8,128)(2,1)} custom-call(bf16[4096,128]{1,0:T(8,128)(2,1)} %bitcast.1, bf16[2,128,128]{2,1,0:T(8,128)(2,1)} %amp.1, s32[2,13]{1,0:T(2,128)} %lstep.1, s32[2,13]{1,0:T(2,128)} %rstep.1, s32[2,13]{1,0:T(2,128)} %own.1, s32[2,13]{1,0:T(2,128)} %slot.1), custom_call_target="tpu_custom_call" | custom-call | flops 4000000000 | bytes 4194304 | tf_op jit(solution)/shard_map/pallas_call | solution.py:320
  47.9 1.3 %copy.8 = bf16[2,32,128]{2,1,0:T(8,128)(2,1)} copy(bf16[2,32,128]{2,1,0:T(8,128)(2,1)} %shard_map.64) | data formatting | bytes 32768
